TPU v7x, 32 devices: a whole 2x2x4 slice. The times are simulated.
32 devices in a mesh: ctx: 4 (over y, x), tp: 8 (over z, core).
Axes of the slice: x: 2, y: 2, z: 4, core: 2. Of those that a mesh axis runs over, the one named last changes fastest.
Arguments:
- resid_in: bfloat16 [512, 1024], P('ctx', 'tp'), may hold values from -6 to 6
- feats: bfloat16 [512, 3, 1024], P('ctx', None, 'tp'), may hold values from -6 to 6
- short_filter: float32 [3, 3, 1024], P(None, None, 'tp'), may hold values from -3.5 to 3.5
- residues: float32 [1024, 16], P('tp'), may hold values from -4 to 4
- rates: float32 [1024, 16], P('tp'), may hold values from 0.0005859375 to 0.03
- out_weight: bfloat16 [1024, 1024], P('tp'), may hold values from -0.25 to 0.25
- norm_gain: float32 [1024], replicated, may hold values from 0.1 to 1.9
- attn_weight: bfloat16 [1024, 3, 1024], P(None, None, 'tp'), may hold values from -1 to 1
Outputs:
- hyena_out: bfloat16 [512, 1024], P('ctx', 'tp')
- context: bfloat16 [512, 1024], P('ctx', 'tp')
All inputs are finite; a program needn't handle non-finite values.
Results may differ from a plain program's by a relative error of at most 0.01.
Values may be sent and summed in bfloat16 or wider, within the bound.
A program may use at most 192 MiB of HBM per device.

v0:
```python
import math

import jax
import jax.numpy as jnp
from jax import lax
from jax.sharding import PartitionSpec as P

HEAD_DIM = 128


eps_norm = 1e-05
rope_base = 10000.0
mask_fill = -1e30
highest = lax.Precision.HIGHEST


def shifted(value, axis, steps):
    count = lax.axis_size(axis)
    initial, last = (max(0, -steps), min(count, count - steps))
    return lax.ppermute(value, axis, [(source, source + steps) for source in range(initial, last)])


def toeplitz_lower(filter_taps):
    chan_count, block_size = filter_taps.shape
    padded = jnp.concatenate(
        [jnp.zeros((chan_count, block_size - 1), jnp.float32), filter_taps], axis=1
    )
    flipped = padded[:, ::-1]
    tiled = jnp.tile(flipped, (1, block_size))
    offset = block_size - 1
    window = tiled[:, offset : offset + block_size * (2 * block_size - 2)]
    return window.reshape(chan_count, block_size, 2 * block_size - 2)[:, :, :block_size]


def modal_conv(signal, residues, rates, start_state):
    chan_count, length = signal.shape
    block_size = math.gcd(length, 128)
    block_count = length // block_size
    weight = residues * jnp.sqrt(1.0 - jnp.exp(-2.0 * rates))
    lag_steps = jnp.arange(block_size, dtype=jnp.float32)
    powers = jnp.exp(-rates[:, :, None] * lag_steps)
    filter_taps = jnp.sum(weight[:, :, None] * powers, axis=1)
    toeplitz = toeplitz_lower(filter_taps)
    blocks = signal.reshape(chan_count, block_count, block_size)
    inner_part = jnp.einsum("cij,cnj->cni", toeplitz, blocks, precision=highest)
    tail_powers = jnp.exp(-rates[:, :, None] * (block_size - lag_steps))
    end_states = jnp.einsum("cnj,cmj->cnm", blocks, tail_powers, precision=highest)
    block_steps = jnp.arange(block_count, dtype=jnp.float32)
    gap_count = block_steps[:, None] - 1.0 - block_steps[None, :]
    live_mask = gap_count >= 0.0
    carry_mat = jnp.where(
        live_mask, jnp.exp(-rates[:, :, None, None] * block_size * jnp.maximum(gap_count, 0.0)), 0.0
    )
    states = jnp.einsum("cmnk,ckm->cnm", carry_mat, end_states, precision=highest)
    states = (
        states
        + jnp.exp(-rates[:, None, :] * block_size * block_steps[None, :, None])
        * start_state[:, None, :]
    )
    cross_part = jnp.einsum("cnm,cmi->cni", states * weight[:, None, :], powers, precision=highest)
    return (inner_part + cross_part).reshape(chan_count, length)


def short_mix(feats, short_filter):
    row_count = feats.shape[0]
    prior_feats = shifted(feats[-2:], "ctx", 1)
    joined = jnp.concatenate([prior_feats, feats], axis=0).astype(jnp.float32)
    return (
        short_filter[0] * joined[2:]
        + short_filter[1] * joined[1 : row_count + 1]
        + short_filter[2] * joined[:row_count]
    )


def rotary_turn(vectors, positions):
    half_dim = vectors.shape[-1] // 2
    frequency = rope_base ** (-jnp.arange(half_dim, dtype=jnp.float32) * 2.0 / vectors.shape[-1])
    angles = positions.astype(jnp.float32)[:, None] * frequency[None, :]
    cosine = jnp.cos(angles)[:, None, :]
    sine_part = jnp.sin(angles)[:, None, :]
    first_half = vectors[..., :half_dim]
    second = vectors[..., half_dim:]
    return jnp.concatenate(
        [first_half * cosine - second * sine_part, second * cosine + first_half * sine_part],
        axis=-1,
    )


def attend_tile(running, query_rows, query_pos, key_block, value_block, key_start):
    run_peak, denom, accumulated = running
    block_size = key_block.shape[0]
    score_scale = 1.0 / math.sqrt(key_block.shape[2])
    key_pos = key_start + jnp.arange(block_size, dtype=jnp.int32)
    scores = (
        jnp.einsum("shd,khd->hsk", query_rows, key_block, preferred_element_type=jnp.float32)
        * score_scale
    )
    allowed = (query_pos[:, None] >= key_pos[None, :])[None]
    masked = jnp.where(allowed, scores, mask_fill)
    new_peak = jnp.maximum(run_peak, jnp.max(masked, axis=2))
    weights = jnp.where(allowed, jnp.exp(masked - new_peak[:, :, None]), 0.0)
    factor = jnp.exp(run_peak - new_peak)
    denom = denom * factor + jnp.sum(weights, axis=2)
    accumulated = accumulated * factor[:, :, None] + jnp.einsum(
        "hsk,khd->hsd",
        weights.astype(jnp.bfloat16),
        value_block,
        preferred_element_type=jnp.float32,
    )
    return (new_peak, denom, accumulated)


def empty_state(head_count, rows):
    return (
        jnp.full((head_count, rows), mask_fill, jnp.float32),
        jnp.zeros((head_count, rows), jnp.float32),
        jnp.zeros((head_count, rows, HEAD_DIM), jnp.float32),
    )


def finish_rows(state):
    run_peak, denom, accumulated = state
    heads_out = accumulated / denom[:, :, None]
    rows = heads_out.shape[1]
    return (
        heads_out.transpose(1, 0, 2)
        .reshape(rows, heads_out.shape[0] * heads_out.shape[2])
        .astype(jnp.bfloat16)
    )


def per_device(resid_in, feats, short_filter, residues, rates, out_weight, norm_gain, attn_weight):
    row_count, chan_count = resid_in.shape
    width_all = out_weight.shape[1]
    short_out = short_mix(feats, short_filter)
    product = (short_out[:, 1] * short_out[:, 2]).astype(jnp.bfloat16)
    panel_rows = lax.all_to_all(product.T, "ctx", split_axis=0, concat_axis=1, tiled=True)
    panel_count = chan_count // lax.axis_size("ctx")
    panel_start = lax.axis_index("ctx") * panel_count
    panel_res = lax.dynamic_slice_in_dim(residues, panel_start, panel_count, 0)
    panel_rates = lax.dynamic_slice_in_dim(rates, panel_start, panel_count, 0)
    panel_conv = modal_conv(
        panel_rows.astype(jnp.float32), panel_res, panel_rates, jnp.zeros_like(panel_rates)
    )
    returned = lax.all_to_all(panel_conv, "ctx", split_axis=1, concat_axis=0, tiled=True)
    conv_out = returned.T
    gated = (short_out[:, 0] * conv_out).astype(jnp.bfloat16)
    own_share = lax.psum_scatter(
        lax.dot_general(
            out_weight, gated, (((0,), (1,)), ((), ())), preferred_element_type=jnp.float32
        ),
        "tp",
        scatter_dimension=0,
        tiled=True,
    )
    hyena_out = (resid_in.astype(jnp.float32) + own_share.T).astype(jnp.bfloat16)
    full_rows = lax.all_gather(hyena_out, "tp", axis=1, tiled=True)
    wide = full_rows.astype(jnp.float32)
    mean_square = jnp.mean(wide * wide, axis=1, keepdims=True)
    normed = (wide * lax.rsqrt(mean_square + eps_norm) * norm_gain).astype(jnp.bfloat16)
    projected = jnp.dot(
        normed, attn_weight.reshape(width_all, 3 * chan_count), preferred_element_type=jnp.float32
    ).reshape(row_count, 3, chan_count)
    head_count = chan_count // HEAD_DIM
    ctx_index = lax.axis_index("ctx")
    first_pos = ctx_index * row_count
    positions = first_pos + jnp.arange(row_count, dtype=jnp.int32)
    queries = rotary_turn(
        projected[:, 0].reshape(row_count, head_count, HEAD_DIM), positions
    ).astype(jnp.bfloat16)
    keys_all = rotary_turn(
        projected[:, 1].reshape(row_count, head_count, HEAD_DIM), positions
    ).astype(jnp.bfloat16)
    values = projected[:, 2].astype(jnp.bfloat16)
    key_pieces = (keys_all.reshape(row_count, chan_count), values)
    initial = empty_state(head_count, row_count)
    key_rows = lax.all_gather(key_pieces[0], "ctx", axis=0, tiled=True)
    value_rows = lax.all_gather(key_pieces[1], "ctx", axis=0, tiled=True)
    key_total = key_rows.shape[0]
    tiles_block_size = math.gcd(key_total, 1024)
    block_count = key_total // tiles_block_size
    key_blocks = key_rows.reshape(block_count, tiles_block_size, head_count, HEAD_DIM)
    value_blocks = value_rows.reshape(block_count, tiles_block_size, head_count, HEAD_DIM)
    key_blocks, value_blocks, block_ids, block_size = (
        key_blocks,
        value_blocks,
        jnp.arange(block_count, dtype=jnp.int32),
        tiles_block_size,
    )

    def one_tile(carried, slot_item):
        key_block, value_block, block_index = slot_item
        key_start = block_index * block_size
        updated = attend_tile(carried, queries, positions, key_block, value_block, key_start)
        return (updated, None)

    result, _ = lax.scan(one_tile, initial, (key_blocks, value_blocks, block_ids))
    context = finish_rows(result)
    return (hyena_out, context)


def solution(mesh):
    in_specs = (
        P("ctx", "tp"),
        P("ctx", None, "tp"),
        P(None, None, "tp"),
        P("tp", None),
        P("tp", None),
        P("tp", None),
        P(),
        P(None, None, "tp"),
    )
    out_specs = (P("ctx", "tp"), P("ctx", "tp"))
    return jax.shard_map(
        per_device, mesh=mesh, in_specs=in_specs, out_specs=out_specs, check_vma=False
    )
```

profile of v0, /device:TPU:0, one launch (start us, length us, event | category | flops | bytes accessed | tf_op | source)
XLA Modules:
  0.0 130.1 jit_solution(925950872863049188)
XLA Ops:
  7.2 0.0 copy-start
  7.2 0.7 slice.59
  7.9 0.2 copy.25
  8.1 4.8 %collective-permute-start = (bf16[2,3,128]{0,2,1:T(8,128)(2,1)S(1)}, bf16[2,3,128]{0,2,1:T(8,128)(2,1)S(1)}, u32[]{:S(2)}, u32[]{:S(2)}) collective-permute-start(bf16[2,3,128]{0,2,1:T(8,128)(2,1)S(1)} %copy.25), channel_id=1, source_target_pairs={{0,8},{8,16},{16,24},{1,9},{9,17},{17,25},{2,10},{10,18},{18,26},{... | collective-permute-start | bytes 4616 | tf_op jit(solution)/shard_map/ppermute | solution.py:20
  13.0 0.1 fusion.72
  13.0 0.1 fusion.73
  13.1 0.8 broadcast_multiply_fusion
  13.9 0.1 copy.29
  14.0 0.7 slice_bitcast_fusion.3
  14.7 0.1 copy.28
  14.8 0.2 multiply_reduce_fusion.1
  15.0 1.0 copy.26
  16.0 0.0 collective-permute-done
  16.0 0.1 maximum_convert_fusion
  16.2 0.3 fusion.22
  16.5 0.6 fusion.32
  17.1 3.7 %all-to-all-start = ((bf16[4,32,128]{2,1,0:T(8,128)(2,1)}), bf16[4,32,128]{2,1,0:T(8,128)(2,1)S(1)}, u32[]{:S(2)}, u32[]{:S(2)}) async-start(bf16[4,32,128]{2,1,0:T(8,128)(2,1)} %bitcast.8), calls=%async_computation | async-start | bytes 65536 | tf_op jit(solution)/shard_map/all_to_all | solution.py:137
  20.9 0.0 reduce-scatter.2.cloned.1.call-start
  20.9 0.1 copy.30
  20.9 0.1 concatenate.29
  21.0 0.1 reverse
  21.2 0.1 slice.140
  21.2 2.3 %tile.4 = f32[32,128,255]{2,1,0:T(8,128)} broadcast(f32[32,255]{1,0:T(8,128)S(1)} %slice.140), dimensions={0,2} | broadcast | bytes 4210560 | tf_op jit(solution)/shard_map/tile | solution.py:29
  23.5 5.2 %tile.10 = f32[32,32640]{1,0:T(8,128)} reshape(f32[32,128,255]{2,1,0:T(8,128)} %tile.4) | data formatting | bytes 8355840 | tf_op jit(solution)/shard_map/tile | solution.py:29
  28.7 5.3 %slice.81 = f32[32,32512]{1,0:T(8,128)} slice(f32[32,32640]{1,0:T(8,128)} %tile.10), slice={[0:32], [127:32639]} | slice | bytes 8323072 | tf_op jit(solution)/shard_map/slice | solution.py:31
  34.0 9.3 %reshape.256 = f32[32,128,254]{2,1,0:T(8,128)} reshape(f32[32,32512]{1,0:T(8,128)} %slice.81) | data formatting | bytes 8323072 | tf_op jit(solution)/shard_map/reshape | solution.py:32
  43.3 0.0 copy-start.1
  43.3 0.0 copy-start.3
  43.3 0.0 copy-start.4
  43.3 0.0 all-to-all-done
  43.3 0.4 convolution_bitcast_fusion.1
  43.7 0.3 copy.42
  44.0 1.3 %multiply_reduce_fusion = f32[32,16,4]{2,1,0:T(8,128)S(1)} fusion(f32[32,16,4]{2,1,0:T(8,128)S(1)} %copy.42, f32[4,4]{1,0:T(4,128)S(1)} %fusion.72, f32[32,16]{1,0:T(8,128)S(1)} %copy.30, pred[4,4]{1,0:T(4,128)(4,1)S(1)} %fusion.73), kind=kLoop, calls=%fused_computation.10 | loop fusion | flops 30720 | bytes 18512
  45.3 0.2 copy.41
  45.6 0.5 fusion.19
  46.1 3.3 %fusion.3 = f32[32,4,128]{2,1,0:T(4,128)S(1)} fusion(f32[32,4,128]{2,1,0:T(4,128)S(1)} %fusion.19, f32[32,128,254]{2,1,0:T(8,128)} %reshape.256, bf16[4,32,128]{2,1,0:T(8,128)(2,1)S(1)} %all-to-all-done), kind=kOutput, calls=%fused_computation.5 | convolution fusion | flops 25182208 | bytes 2260992 | tf_op jit(solution)/shard_map/cij,cnj->cni/dot_general | solution.py:45
  49.4 8.8 %all_to_all.32 = f32[32,4,128]{2,0,1:T(8,128)S(1)} all-to-all(f32[32,4,128]{2,0,1:T(8,128)S(1)} %copy.33), channel_id=1, replica_groups=mesh['ctx'=4,'tp'=8] {'ctx'}, dimensions={1} | all-to-all | bytes 131072 | tf_op jit(solution)/shard_map/all_to_all | solution.py:145
  58.3 0.0 copy-done
  58.3 1.0 convolution_bitcast_fusion
  59.3 0.0 reduce-scatter.2.cloned.1.call-update
  59.3 0.0 copy-done.1
  59.3 0.3 copy.34
  59.7 30.3 %reduce-scatter.2.cloned.1.call-done = f32[128,128]{0,1:T(8,128)} async-done(((f32[1024,128]{0,1:T(8,128)}), f32[128,128]{0,1:T(8,128)}) %reduce-scatter.2.cloned.1.call-update) | async-done | bytes 65552 | tf_op jit(solution)/shard_map/reduce_scatter | solution.py:148
  90.0 0.0 copy-done.3
  90.0 0.8 fusion.35
  90.9 0.0 copy-start.2
  90.9 13.1 %all_gather.9 = bf16[128,1024]{1,0:T(8,128)(2,1)S(1)} all-gather(bf16[128,128]{1,0:T(8,128)(2,1)S(1)} %fusion.35), channel_id=1, replica_groups=mesh['ctx'=4,'tp'=8] {'tp'}, dimensions={1}, use_global_device_ids=true | all-gather | bytes 294912 | tf_op jit(solution)/shard_map/all_gather | solution.py:157
  104.0 0.1 fusion.10
  104.1 0.0 copy-done.4
  104.1 0.5 fusion.8
  104.6 0.2 fusion.71
  104.8 8.4 %all_gather.10 = bf16[512,128]{0,1:T(8,128)(2,1)S(1)} all-gather(bf16[128,128]{0,1:T(8,128)(2,1)S(1)} %pad_maximum_fusion), channel_id=1, replica_groups=mesh['ctx'=4,'tp'=8] {'ctx'}, dimensions={0}, use_global_device_ids=true | all-gather | bytes 163840 | tf_op jit(solution)/shard_map/all_gather | solution.py:177
  113.2 0.3 fusion.79
  113.5 0.2 fusion.20
  113.8 8.6 %all-gather = bf16[512,1,128]{0,2,1:T(8,128)(2,1)S(1)} all-gather(bf16[128,1,128]{0,2,1:T(8,128)(2,1)S(1)} %slice.141), channel_id=2, replica_groups=mesh['ctx'=4,'tp'=8] {'ctx'}, dimensions={0}, use_global_device_ids=true | all-gather | bytes 163840 | tf_op jit(solution)/shard_map/all_gather | solution.py:178
  122.4 0.9 fusion.7
  123.3 0.0 copy-done.2
  (12 shorter events, 0.1 us)
Async XLA Ops:
  7.2 51.1 %copy-start = (bf16[128,1024]{1,0:T(8,128)(2,1)S(1)}, bf16[128,1024]{1,0:T(8,128)(2,1)}, u32[]{:S(2)}) copy-start(bf16[128,1024]{1,0:T(8,128)(2,1)} %param.13) | copy-start | bytes 786436
  8.1 7.9 %collective-permute-start = (bf16[2,3,128]{0,2,1:T(8,128)(2,1)S(1)}, bf16[2,3,128]{0,2,1:T(8,128)(2,1)S(1)}, u32[]{:S(2)}, u32[]{:S(2)}) collective-permute-start(bf16[2,3,128]{0,2,1:T(8,128)(2,1)S(1)} %copy.25), channel_id=1, source_target_pairs={{0,8},{8,16},{16,24},{1,9},{9,17},{17,25},{2,10},{10,18},{18,26},{... | collective-permute-start | bytes 4616 | tf_op jit(solution)/shard_map/ppermute | solution.py:20
  17.1 26.2 %all-to-all-start = ((bf16[4,32,128]{2,1,0:T(8,128)(2,1)}), bf16[4,32,128]{2,1,0:T(8,128)(2,1)S(1)}, u32[]{:S(2)}, u32[]{:S(2)}) async-start(bf16[4,32,128]{2,1,0:T(8,128)(2,1)} %bitcast.8), calls=%async_computation | async-start | bytes 65536 | tf_op jit(solution)/shard_map/all_to_all | solution.py:137
  20.9 69.1 %reduce-scatter.2.cloned.1.call-start = ((), (), s32[]{:S(2)}) async-start(), calls=%async_computation.3 | async-start | bytes 589824 | tf_op jit(solution)/shard_map/reduce_scatter | solution.py:148
  43.3 16.0 %copy-start.1 = (bf16[1024,3,128]{2,0,1:T(8,128)(2,1)S(1)}, bf16[1024,3,128]{2,0,1:T(8,128)(2,1)}, u32[]{:S(2)}) copy-start(bf16[1024,3,128]{2,0,1:T(8,128)(2,1)} %param.15) | copy-start | bytes 2359300
  43.3 46.7 %copy-start.3 = (bf16[128,128]{1,0:T(8,128)(2,1)S(1)}, bf16[128,128]{1,0:T(8,128)(2,1)}, u32[]{:S(2)}) copy-start(bf16[128,128]{1,0:T(8,128)(2,1)} %param.8) | copy-start | bytes 98308
  43.3 60.8 %copy-start.4 = (f32[1024]{0:T(1024)S(1)}, f32[1024]{0:T(1024)}, u32[]{:S(2)}) copy-start(f32[1024]{0:T(1024)} %param.14) | copy-start | bytes 12292
  90.9 32.4 %copy-start.2 = (bf16[128,128]{1,0:T(8,128)(2,1)}, bf16[128,128]{1,0:T(8,128)(2,1)S(1)}, u32[]{:S(2)}) copy-start(bf16[128,128]{1,0:T(8,128)(2,1)S(1)} %fusion.35) | copy-start | bytes 98308
Sparse Core Ops, SparseCore 0:
  59.5 30.5 reduce-scatter.1
where the time goes:
time: 131 us; the launch traced here: 130 us
  blocking collectives  39 us (30%)
  waiting for transfers between devices  30.3 us (23%)
  local copies, waits for them, and re-layouts  26.1 us (20%)
  between operations  14.2 us (11%)
  starting transfers between devices  8.59 us (7%)
  matrix products  6.84 us (5%)
  other arithmetic  5.05 us (4%)
    reduce_scatter x1, waiting for transfers between devices, per_device(): lax.psum_scatter(lax.dot_general(out_weight, gated, (((0,), (1,)), ((), (...  30.3 us
    all_gather x1, blocking collectives, per_device(): full_rows = lax.all_gather(hyena_out, 'tp', axis=1, tiled=True)  13.1 us
    reshape x1, local copies, waits for them, and re-layouts, toeplitz_lower(): window.reshape(chan_count, block_size, 2 * block_size - 2)  9.27 us
    all_to_all x1, blocking collectives, per_device(): lax.all_to_all(panel_conv, 'ctx', split_axis=1, concat_axis=0, tiled=True)  8.84 us
    all_gather x1, blocking collectives, per_device(): value_rows = lax.all_gather(key_pieces[1], 'ctx', axis=0, tiled=True)  8.63 us
    all_gather x1, blocking collectives, per_device(): key_rows = lax.all_gather(key_pieces[0], 'ctx', axis=0, tiled=True)  8.42 us
    another operation x2, local copies, waits for them, and re-layouts, toeplitz_lower(): tiled = jnp.tile(flipped, (1, block_size))  7.5 us
    slice x1, local copies, waits for them, and re-layouts, toeplitz_lower(): window = tiled[:, offset:offset + block_size * (2 * block_size - 2)]  5.29 us
  transfers between devices with their start and end apart: 3, of which 1 were waited for; matrix products, arithmetic and copies ran while one was open for 20% of the time, Pallas kernels for 0%

commit v1 on v0

v1 whole, which is shorter than its diff:
```python
import functools
import math

import jax
import jax.numpy as jnp
import numpy as np
from jax import lax
from jax.experimental import pallas as pl
from jax.experimental.pallas import tpu as pltpu
from jax.sharding import PartitionSpec as P

HEAD_DIM = 128
EPS = 1e-05
ROPE_BASE = 10000.0
FILL = -1e30
MESH = pl.DeviceIdType.MESH
F32 = jnp.float32
BF16 = jnp.bfloat16


def kernel(
    n_ctx,
    n_tp,
    resid_ref,
    feats_ref,
    sf_ref,
    res_ref,
    rate_ref,
    gain_ref,
    table_ref,
    base_ref,
    ow_hbm,
    aw_hbm,
    hy_ref,
    ctx_ref,
    ow,
    aw,
    xpad,
    prod,
    fsh,
    msg,
    msg_in,
    part_out,
    part_in,
    gath,
    kv,
    scores,
    w_sem,
    s1,
    r1,
    s2,
    r2,
    s3,
    r3,
    s4,
    r4,
):
    me_c = lax.axis_index("ctx")
    me_t = lax.axis_index("tp")
    rows = resid_ref.shape[0]
    modes = res_ref.shape[0]
    width = n_tp * 128
    tiles = rows // 8

    barrier = pltpu.get_barrier_semaphore()
    for d in range(1, n_tp):
        peer = lax.rem(me_t + d, n_tp)
        pl.semaphore_signal(barrier, inc=1, device_id={"tp": peer}, device_id_type=MESH)
    for d in range(1, n_ctx):

        @pl.when(me_c >= d)
        def _(d=d):
            pl.semaphore_signal(
                barrier, inc=1, device_id={"ctx": me_c - d}, device_id_type=MESH
            )

    w_copies = [pltpu.make_async_copy(ow_hbm, ow, w_sem.at[0])]
    for slot, p in enumerate((1, 2, 0)):
        w_copies.append(
            pltpu.make_async_copy(
                aw_hbm.at[p], aw.at[:, pl.ds(slot * 128, 128)], w_sem.at[1 + slot]
            )
        )
    for c in w_copies:
        c.start()

    short = []
    for p in range(3):
        x = feats_ref[p].astype(F32)
        xpad[p, 0:8, :] = jnp.zeros((8, 128), F32)
        xpad[p, pl.ds(8, rows), :] = x
        short.append(
            sf_ref[0, p : p + 1, :] * x
            + sf_ref[1, p : p + 1, :] * xpad[p, pl.ds(7, rows), :]
            + sf_ref[2, p : p + 1, :] * xpad[p, pl.ds(6, rows), :]
        )
    row_id = lax.broadcasted_iota(jnp.int32, (rows, 128), 0)
    p_mask = jnp.where(row_id >= 2, (short[1] * short[2]).astype(BF16).astype(F32), 0.0)
    prod[...] = p_mask

    rates = rate_ref[...]
    eight = lax.broadcasted_iota(jnp.int32, (8, 128), 0).astype(F32)
    lam8 = jnp.exp(-8.0 * rates)

    for m in range(modes):
        state = p_mask[0:8]
        for i in range(1, tiles):
            state = state * lam8[m : m + 1] + p_mask[8 * i : 8 * i + 8]
        state = state * jnp.exp(-rates[m : m + 1] * (7.0 - eight))
        msg[m : m + 1, :] = jnp.sum(state, axis=0, keepdims=True)
    for p in range(3):
        msg[16 + 2 * p : 18 + 2 * p, :] = xpad[p, rows + 6 : rows + 8, :]
    for p in range(1, 3):
        msg[20 + 2 * p : 22 + 2 * p, :] = xpad[p, 8:10, :]
    msg[26:32, :] = jnp.zeros((6, 128), F32)

    pl.semaphore_wait(barrier, n_tp - 1 + (n_ctx - 1 - me_c))

    def msg_copy(d):
        return pltpu.make_async_remote_copy(
            src_ref=msg,
            dst_ref=msg_in.at[me_c],
            send_sem=s1.at[d],
            recv_sem=r1.at[me_c],
            device_id={"ctx": me_c + d},
            device_id_type=MESH,
        )

    for d in range(1, n_ctx):

        @pl.when(me_c + d < n_ctx)
        def _(d=d):
            msg_copy(d).start()

    weight = res_ref[...] * jnp.sqrt(1.0 - jnp.exp(-2.0 * rates))
    taps = [jnp.zeros((8, 128), F32) for _ in range(tiles)]
    for m in range(modes):
        e = weight[m : m + 1] * jnp.exp(-rates[m : m + 1] * eight)
        for i in range(tiles):
            taps[i] = taps[i] + e
            e = e * lam8[m : m + 1]
    taps = jnp.concatenate(taps, axis=0)
    for r in range(8):
        fsh[r, 0 : rows + 8, :] = jnp.zeros((rows + 8, 128), F32)
        fsh[r, rows + r : 2 * rows, :] = taps[0 : rows - r]

    def conv_step(j, acc):
        start = pl.multiple_of(rows - 8 * j, 8)
        block = prod[pl.ds(pl.multiple_of(8 * j, 8), 8), :]
        for r in range(8):
            acc = acc + fsh[r, pl.ds(start, rows), :] * block[r : r + 1]
        return acc

    conv = lax.fori_loop(0, tiles, conv_step, jnp.zeros((rows, 128), F32))

    cos_l, sin_l = table_ref[0], table_ref[1]
    cos_b = base_ref[0, pl.ds(me_c, 1), :]
    sin_b = base_ref[1, pl.ds(me_c, 1), :]
    lane = lax.broadcasted_iota(jnp.int32, (rows, 128), 1)
    cosine = cos_b * cos_l - sin_b * sin_l
    sine = sin_b * cos_l + cos_b * sin_l
    sine = jnp.where(lane < 64, -sine, sine)

    span = float(rows)
    lam_full = jnp.exp(-span * rates)
    lam_p0 = jnp.exp(-(span - 1.0) * rates)
    lam_p1 = jnp.exp(-(span - 2.0) * rates)

    def tap(j, p):
        return sf_ref[j, p : p + 1, :]

    def first_rows(p, x0, x1, h0, h1):
        a = tap(0, p) * x0 + tap(1, p) * h1 + tap(2, p) * h0
        b = tap(0, p) * x1 + tap(1, p) * x0 + tap(2, p) * h1
        return a, b

    def first_products(kx, vx, halo):
        k0, k1 = first_rows(1, kx[0], kx[1], halo[2], halo[3])
        v0, v1 = first_rows(2, vx[0], vx[1], halo[4], halo[5])
        return (k0 * v0).astype(BF16).astype(F32), (k1 * v1).astype(BF16).astype(F32)

    def state_step(k, carried):
        total, halo = carried
        pltpu.make_async_remote_copy(
            src_ref=msg,
            dst_ref=msg_in.at[k],
            send_sem=s1.at[0],
            recv_sem=r1.at[k],
            device_id={"ctx": k},
            device_id_type=MESH,
        ).wait_recv()
        got = [msg_in[k, i : i + 1, :] for i in range(16, 26)]
        p0, p1 = first_products(got[6:8], got[8:10], halo)
        total = total * lam_full + msg_in[k, 0:modes, :] + lam_p0 * p0 + lam_p1 * p1
        return total, tuple(got[0:6])

    zero_row = jnp.zeros((1, 128), F32)
    total, halo = lax.fori_loop(
        0, me_c, state_step, (jnp.zeros((modes, 128), F32), (zero_row,) * 6)
    )
    p0, p1 = first_products(
        [xpad[1, 8:9, :], xpad[1, 9:10, :]], [xpad[2, 8:9, :], xpad[2, 9:10, :]], halo
    )
    q0, q1 = first_rows(0, xpad[0, 8:9, :], xpad[0, 9:10, :], halo[0], halo[1])
    total = total * weight
    cross = [jnp.zeros((8, 128), F32) for _ in range(tiles)]
    for m in range(modes):
        e = total[m : m + 1] * jnp.exp(-rates[m : m + 1] * (eight + 1.0))
        for i in range(tiles):
            cross[i] = cross[i] + e
            e = e * lam8[m : m + 1]
    conv = conv + jnp.concatenate(cross, axis=0)
    conv = conv + fsh[0, pl.ds(rows, rows), :] * p0 + fsh[1, pl.ds(rows, rows), :] * p1
    query_part = jnp.where(row_id == 0, q0, jnp.where(row_id == 1, q1, short[0]))
    gated = (query_part * conv).astype(BF16)

    w_copies[0].wait()

    def part_copy(d, target):
        return pltpu.make_async_remote_copy(
            src_ref=part_out.at[d],
            dst_ref=part_in.at[d],
            send_sem=s2.at[d],
            recv_sem=r2.at[d],
            device_id={"tp": target},
            device_id_type=MESH,
        )

    def columns(t):
        return ow[:, pl.ds(pl.multiple_of(t * 128, 128), 128)]

    for d in range(1, n_tp):
        peer = lax.rem(me_t + d, n_tp)
        part_out[d] = jnp.dot(gated, columns(peer), preferred_element_type=F32).astype(BF16)
        part_copy(d, peer).start()
    mix = jnp.dot(gated, columns(me_t), preferred_element_type=F32)
    for d in range(1, n_tp):
        part_copy(d, me_t).wait_recv()
        mix = mix + part_in[d].astype(F32)
    hyena = (resid_ref[...].astype(F32) + mix).astype(BF16)
    gath[me_t] = hyena

    def gath_copy(d, owner, target):
        return pltpu.make_async_remote_copy(
            src_ref=gath.at[owner],
            dst_ref=gath.at[owner],
            send_sem=s3.at[d],
            recv_sem=r3.at[d],
            device_id={"tp": target},
            device_id_type=MESH,
        )

    for d in range(1, n_tp):
        gath_copy(d, me_t, lax.rem(me_t + d, n_tp)).start()
    hy_ref[...] = hyena
    for d in range(1, n_tp):
        gath_copy(d, lax.rem(me_t + n_tp - d, n_tp), me_t).wait_recv()
    wide = [gath[j].astype(F32) for j in range(n_tp)]
    square = wide[0] * wide[0]
    for j in range(1, n_tp):
        square = square + wide[j] * wide[j]
    scale = lax.rsqrt(jnp.sum(square, axis=1, keepdims=True) / float(width) + EPS)
    normed = jnp.concatenate(
        [(wide[j] * scale * gain_ref[j : j + 1, :]).astype(BF16) for j in range(n_tp)], axis=1
    )
    for c in w_copies[1:]:
        c.wait()

    def turned(x):
        return (x * cosine + pltpu.roll(x, 64, axis=1) * sine).astype(BF16)

    key_value = jnp.dot(normed, aw[:, 0:256], preferred_element_type=F32)
    kv[0, me_c] = turned(key_value[:, 0:128])
    kv[1, me_c] = key_value[:, 128:256].astype(BF16)

    def kv_copy(which, d, owner, target):
        return pltpu.make_async_remote_copy(
            src_ref=kv.at[which, owner],
            dst_ref=kv.at[which, owner],
            send_sem=s4.at[which, d],
            recv_sem=r4.at[which, owner],
            device_id={"ctx": target},
            device_id_type=MESH,
        )

    for which in range(2):
        for d in range(1, n_ctx):

            @pl.when(me_c + d < n_ctx)
            def _(which=which, d=d):
                kv_copy(which, d, me_c, me_c + d).start()

    queries = turned(jnp.dot(normed, aw[:, 256:384], preferred_element_type=F32))
    factor = 1.0 / math.sqrt(HEAD_DIM)

    def score_of(k):
        return (
            lax.dot_general(
                queries, kv[0, k], (((1,), (1,)), ((), ())), preferred_element_type=F32
            )
            * factor
        )

    own = jnp.where(row_id >= lane, score_of(me_c), FILL)

    def score_step(k, peak):
        kv_copy(0, 0, k, k).wait_recv()
        s = score_of(k)
        scores[k] = s
        return jnp.maximum(peak, s)

    peak = jnp.max(lax.fori_loop(0, me_c, score_step, own), axis=1, keepdims=True)
    probs = jnp.where(row_id >= lane, jnp.exp(own - peak), 0.0)
    acc = jnp.dot(probs.astype(BF16), kv[1, me_c], preferred_element_type=F32)

    def value_step(k, carried):
        total_p, total_v = carried
        kv_copy(1, 0, k, k).wait_recv()
        pr = jnp.exp(scores[k] - peak)
        total_v = total_v + jnp.dot(pr.astype(BF16), kv[1, k], preferred_element_type=F32)
        return total_p + pr, total_v

    probs, acc = lax.fori_loop(0, me_c, value_step, (probs, acc))
    ctx_ref[...] = (acc / jnp.sum(probs, axis=1, keepdims=True)).astype(BF16)

    for d in range(1, n_tp):
        part_copy(d, me_t).wait_send()
        gath_copy(d, me_t, me_t).wait_send()
    for d in range(1, n_ctx):

        @pl.when(me_c + d < n_ctx)
        def _(d=d):
            msg_copy(d).wait_send()
            kv_copy(0, d, me_c, me_c + d).wait_send()
            kv_copy(1, d, me_c, me_c + d).wait_send()


def rotary_tables(rows, n_ctx):
    half = HEAD_DIM // 2
    freq = ROPE_BASE ** (-np.arange(half, dtype=np.float64) * 2.0 / HEAD_DIM)
    freq = np.concatenate([freq, freq])
    local = np.arange(rows)[:, None] * freq
    base = (np.arange(n_ctx) * rows)[:, None] * freq
    table = np.stack([np.cos(local), np.sin(local)]).astype(np.float32)
    return table, np.stack([np.cos(base), np.sin(base)]).astype(np.float32)


def solution(mesh):
    n_ctx, n_tp = mesh.shape["ctx"], mesh.shape["tp"]

    def per_device(resid, feats, sf, residues, rates, ow, gain, aw):
        rows = resid.shape[0]
        width = ow.shape[1]
        table, base = rotary_tables(rows, n_ctx)
        vmem = pl.BlockSpec(memory_space=pltpu.VMEM)
        hbm = pl.BlockSpec(memory_space=pltpu.HBM)
        dma = pltpu.SemaphoreType.DMA
        block = (rows, 128)
        return pl.pallas_call(
            functools.partial(kernel, n_ctx, n_tp),
            out_shape=(
                jax.ShapeDtypeStruct(block, BF16),
                jax.ShapeDtypeStruct(block, BF16),
            ),
            in_specs=[vmem] * 8 + [hbm] * 2,
            out_specs=(vmem, vmem),
            scratch_shapes=[
                pltpu.VMEM(ow.shape, BF16),
                pltpu.VMEM((width, 384), BF16),
                pltpu.VMEM((3, rows + 8, 128), F32),
                pltpu.VMEM(block, F32),
                pltpu.VMEM((8, 2 * rows, 128), F32),
                pltpu.VMEM((32, 128), F32),
                pltpu.VMEM((n_ctx, 32, 128), F32),
                pltpu.VMEM((n_tp,) + block, BF16),
                pltpu.VMEM((n_tp,) + block, BF16),
                pltpu.VMEM((n_tp,) + block, BF16),
                pltpu.VMEM((2, n_ctx) + block, BF16),
                pltpu.VMEM((n_ctx,) + block, F32),
                dma((4,)),
                dma((n_ctx,)),
                dma((n_ctx,)),
                dma((n_tp,)),
                dma((n_tp,)),
                dma((n_tp,)),
                dma((n_tp,)),
                dma((2, n_ctx)),
                dma((2, n_ctx)),
            ],
            compiler_params=pltpu.CompilerParams(
                collective_id=0, has_side_effects=True, vmem_limit_bytes=40 * 1024 * 1024
            ),
        )(
            resid,
            feats.transpose(1, 0, 2),
            sf,
            residues.T,
            rates.T,
            gain.reshape(n_tp, 128),
            jnp.asarray(table),
            jnp.asarray(base),
            ow,
            aw.transpose(1, 0, 2),
        )

    in_specs = (
        P("ctx", "tp"),
        P("ctx", None, "tp"),
        P(None, None, "tp"),
        P("tp", None),
        P("tp", None),
        P("tp", None),
        P(),
        P(None, None, "tp"),
    )
    return jax.shard_map(
        per_device,
        mesh=mesh,
        in_specs=in_specs,
        out_specs=(P("ctx", "tp"), P("ctx", "tp")),
        check_vma=False,
    )
```

time: 131 us -> 34.7 us (0.26)
  the two profiles are of different devices: /device:TPU:0 before, /device:TPU:30 now
where the time goes in v1:
time: 34.7 us; the launch traced here: 34.2 us
  Pallas kernels  24.2 us (70%)
  local copies, waits for them, and re-layouts  9.32 us (27%)
  between operations  0.66 us (2%)
    pallas_call x1, Pallas kernels, per_device(): pl.pallas_call(functools.partial(kernel, n_ctx, n_tp), out_shape=(jax.Sha...  24.2 us
    unnamed x22, local copies, waits for them, and re-layouts  9.32 us

profile of v1, /device:TPU:30, one launch (start us, length us, event | category | flops | bytes accessed | tf_op | source)
XLA Modules:
  0.0 34.2 jit_solution(9059978802168809306)
XLA Ops:
  0.6 0.0 copy-start.5
  0.6 0.7 %copy-done.5 = f32[128,16]{0,1:T(8,128)S(1)} copy-done((f32[128,16]{0,1:T(8,128)S(1)}, f32[128,16]{0,1:T(8,128)}, u32[]{:S(2)}) %copy-start.5) | copy-done | bytes 8216
  1.3 0.0 copy-start
  1.3 1.1 %copy-done = bf16[1024,3,128]{2,0,1:T(8,128)(2,1)S(1)} copy-done((bf16[1024,3,128]{2,0,1:T(8,128)(2,1)S(1)}, bf16[1024,3,128]{2,0,1:T(8,128)(2,1)}, u32[]{:S(2)}) %copy-start) | copy-done | bytes 786456
  2.5 0.0 copy-start.1
  2.5 0.9 %copy-done.1 = bf16[128,1024]{1,0:T(8,128)(2,1)S(1)} copy-done((bf16[128,1024]{1,0:T(8,128)(2,1)S(1)}, bf16[128,1024]{1,0:T(8,128)(2,1)}, u32[]{:S(2)}) %copy-start.1) | copy-done | bytes 262168
  3.4 0.0 copy-start.2
  3.4 0.9 %copy-done.2 = f32[2,128,128]{2,1,0:T(8,128)S(1)} copy-done((f32[2,128,128]{2,1,0:T(8,128)S(1)}, f32[2,128,128]{2,1,0:T(8,128)}, u32[]{:S(2)}) %copy-start.2) | copy-done | bytes 131096
  4.3 0.0 copy-start.3
  4.3 0.9 %copy-done.3 = bf16[128,3,128]{2,0,1:T(8,128)(2,1)S(1)} copy-done((bf16[128,3,128]{2,0,1:T(8,128)(2,1)S(1)}, bf16[128,3,128]{2,0,1:T(8,128)(2,1)}, u32[]{:S(2)}) %copy-start.3) | copy-done | bytes 98328
  5.2 0.0 copy-start.4
  5.2 0.8 %copy-done.4 = bf16[128,128]{1,0:T(8,128)(2,1)S(1)} copy-done((bf16[128,128]{1,0:T(8,128)(2,1)S(1)}, bf16[128,128]{1,0:T(8,128)(2,1)}, u32[]{:S(2)}) %copy-start.4) | copy-done | bytes 32792
  6.0 0.0 copy-start.6
  6.0 0.7 %copy-done.6 = f32[128,16]{0,1:T(8,128)S(1)} copy-done((f32[128,16]{0,1:T(8,128)S(1)}, f32[128,16]{0,1:T(8,128)}, u32[]{:S(2)}) %copy-start.6) | copy-done | bytes 8216
  6.7 0.0 copy-start.7
  6.7 0.7 %copy-done.7 = f32[3,3,128]{2,1,0:T(4,128)S(1)} copy-done((f32[3,3,128]{2,1,0:T(4,128)S(1)}, f32[3,3,128]{2,1,0:T(4,128)}, u32[]{:S(2)}) %copy-start.7) | copy-done | bytes 4632
  7.4 0.0 copy-start.8
  7.4 0.7 %copy-done.8 = f32[1024]{0:T(1024)S(1)} copy-done((f32[1024]{0:T(1024)S(1)}, f32[1024]{0:T(1024)}, u32[]{:S(2)}) %copy-start.8) | copy-done | bytes 4120
  8.0 0.0 copy-start.9
  8.1 0.7 %copy-done.9 = f32[2,4,128]{2,1,0:T(4,128)S(1)} copy-done((f32[2,4,128]{2,1,0:T(4,128)S(1)}, f32[2,4,128]{2,1,0:T(4,128)}, u32[]{:S(2)}) %copy-start.9) | copy-done | bytes 4120
  8.7 24.2 %shard_map.113 = (bf16[128,128]{1,0:T(8,128)(2,1)S(1)}, bf16[128,128]{1,0:T(8,128)(2,1)S(1)}) custom-call(bf16[128,128]{1,0:T(8,128)(2,1)S(1)} %copy-done.4, bf16[3,128,128]{2,1,0:T(8,128)(2,1)S(1)} %bitcast.6, f32[3,3,128]{2,1,0:T(4,128)S(1)} %copy-done.7, f32[16,128]{1,0:T(8,128)S(1)} %bitcast.7, f32[16,128]{1,0:T(8,128)S(1)} %bitcast.8, ...), custom_call_target="tpu_custom_call" | custom-call | tf_op jit(solution)/shard_map/pallas_call | solution.py:359
  33.0 0.6 %copy.14 = bf16[128,128]{1,0:T(8,128)(2,1)} copy(bf16[128,128]{1,0:T(8,128)(2,1)S(1)} %get-tuple-element.4) | data formatting | bytes 65536
  33.6 0.6 %copy.15 = bf16[128,128]{1,0:T(8,128)(2,1)} copy(bf16[128,128]{1,0:T(8,128)(2,1)S(1)} %get-tuple-element.5) | data formatting | bytes 65536
Async XLA Ops:
  0.6 0.7 %copy-start.5 = (f32[128,16]{0,1:T(8,128)S(1)}, f32[128,16]{0,1:T(8,128)}, u32[]{:S(2)}) copy-start(f32[128,16]{0,1:T(8,128)} %param.13) | copy-start | bytes 24580
  1.3 1.1 %copy-start = (bf16[1024,3,128]{2,0,1:T(8,128)(2,1)S(1)}, bf16[1024,3,128]{2,0,1:T(8,128)(2,1)}, u32[]{:S(2)}) copy-start(bf16[1024,3,128]{2,0,1:T(8,128)(2,1)} %param.17) | copy-start | bytes 2359300
  2.5 0.9 %copy-start.1 = (bf16[128,1024]{1,0:T(8,128)(2,1)S(1)}, bf16[128,1024]{1,0:T(8,128)(2,1)}, u32[]{:S(2)}) copy-start(bf16[128,1024]{1,0:T(8,128)(2,1)} %ow_hbm.1) | copy-start | bytes 786436
  3.4 0.9 %copy-start.2 = (f32[2,128,128]{2,1,0:T(8,128)S(1)}, f32[2,128,128]{2,1,0:T(8,128)}, u32[]{:S(2)}) copy-start(f32[2,128,128]{2,1,0:T(8,128)} %constant.4.clone.table_ref) | copy-start | bytes 393220
  4.3 0.9 %copy-start.3 = (bf16[128,3,128]{2,0,1:T(8,128)(2,1)S(1)}, bf16[128,3,128]{2,0,1:T(8,128)(2,1)}, u32[]{:S(2)}) copy-start(bf16[128,3,128]{2,0,1:T(8,128)(2,1)} %param.11) | copy-start | bytes 294916
  5.2 0.8 %copy-start.4 = (bf16[128,128]{1,0:T(8,128)(2,1)S(1)}, bf16[128,128]{1,0:T(8,128)(2,1)}, u32[]{:S(2)}) copy-start(bf16[128,128]{1,0:T(8,128)(2,1)} %resid_ref.1) | copy-start | bytes 98308
  6.0 0.7 %copy-start.6 = (f32[128,16]{0,1:T(8,128)S(1)}, f32[128,16]{0,1:T(8,128)}, u32[]{:S(2)}) copy-start(f32[128,16]{0,1:T(8,128)} %param.14) | copy-start | bytes 24580
  6.7 0.7 %copy-start.7 = (f32[3,3,128]{2,1,0:T(4,128)S(1)}, f32[3,3,128]{2,1,0:T(4,128)}, u32[]{:S(2)}) copy-start(f32[3,3,128]{2,1,0:T(4,128)} %sf_ref.1) | copy-start | bytes 13828
  7.4 0.7 %copy-start.8 = (f32[1024]{0:T(1024)S(1)}, f32[1024]{0:T(1024)}, u32[]{:S(2)}) copy-start(f32[1024]{0:T(1024)} %param.16) | copy-start | bytes 12292
  8.0 0.7 %copy-start.9 = (f32[2,4,128]{2,1,0:T(4,128)S(1)}, f32[2,4,128]{2,1,0:T(4,128)}, u32[]{:S(2)}) copy-start(f32[2,4,128]{2,1,0:T(4,128)} %constant.5.clone.base_ref) | copy-start | bytes 12292

commit v2 on v1

--- a/solution.py
+++ b/solution.py
@@ -21,6 +21,18 @@
 def kernel(
     n_ctx,
     n_tp,
+    resid_hbm,
+    feats_hbm,
+    sf_hbm,
+    res_hbm,
+    rate_hbm,
+    gain_hbm,
+    table_hbm,
+    base_hbm,
+    ow_hbm,
+    aw_hbm,
+    hy_ref,
+    ctx_ref,
     resid_ref,
     feats_ref,
     sf_ref,
@@ -29,10 +41,6 @@
     gain_ref,
     table_ref,
     base_ref,
-    ow_hbm,
-    aw_hbm,
-    hy_ref,
-    ctx_ref,
     ow,
     aw,
     xpad,
@@ -46,6 +54,7 @@
     kv,
     scores,
     w_sem,
+    in_sem,
     s1,
     r1,
     s2,
@@ -62,6 +71,23 @@
     width = n_tp * 128
     tiles = rows // 8
 
+    in_copies = []
+    for i, (src, dst) in enumerate(
+        (
+            (feats_hbm, feats_ref),
+            (sf_hbm, sf_ref),
+            (rate_hbm, rate_ref),
+            (res_hbm, res_ref),
+            (table_hbm, table_ref),
+            (base_hbm, base_ref),
+            (resid_hbm, resid_ref),
+            (gain_hbm, gain_ref),
+        )
+    ):
+        in_copies.append(pltpu.make_async_copy(src, dst, in_sem.at[i]))
+    for c in in_copies:
+        c.start()
+
     barrier = pltpu.get_barrier_semaphore()
     for d in range(1, n_tp):
         peer = lax.rem(me_t + d, n_tp)
@@ -83,6 +109,9 @@
         )
     for c in w_copies:
         c.start()
+
+    for c in in_copies[0:3]:
+        c.wait()
 
     short = []
     for p in range(3):
@@ -132,6 +161,8 @@
         def _(d=d):
             msg_copy(d).start()
 
+    for c in in_copies[3:]:
+        c.wait()
     weight = res_ref[...] * jnp.sqrt(1.0 - jnp.exp(-2.0 * rates))
     taps = [jnp.zeros((8, 128), F32) for _ in range(tiles)]
     for m in range(modes):
@@ -359,12 +390,20 @@
         return pl.pallas_call(
             functools.partial(kernel, n_ctx, n_tp),
             out_shape=(
-                jax.ShapeDtypeStruct(block, BF16),
-                jax.ShapeDtypeStruct(block, BF16),
+                pltpu.VMEM(block, BF16),
+                pltpu.VMEM(block, BF16),
             ),
-            in_specs=[vmem] * 8 + [hbm] * 2,
+            in_specs=[hbm] * 10,
             out_specs=(vmem, vmem),
             scratch_shapes=[
+                pltpu.VMEM(block, BF16),
+                pltpu.VMEM((3,) + block, BF16),
+                pltpu.VMEM(sf.shape, F32),
+                pltpu.VMEM(residues.shape[::-1], F32),
+                pltpu.VMEM(rates.shape[::-1], F32),
+                pltpu.VMEM((n_tp, 128), F32),
+                pltpu.VMEM(table.shape, F32),
+                pltpu.VMEM(base.shape, F32),
                 pltpu.VMEM(ow.shape, BF16),
                 pltpu.VMEM((width, 384), BF16),
                 pltpu.VMEM((3, rows + 8, 128), F32),
@@ -378,6 +417,7 @@
                 pltpu.VMEM((2, n_ctx) + block, BF16),
                 pltpu.VMEM((n_ctx,) + block, F32),
                 dma((4,)),
+                dma((8,)),
                 dma((n_ctx,)),
                 dma((n_ctx,)),
                 dma((n_tp,)),
@@ -388,7 +428,7 @@
                 dma((2, n_ctx)),
             ],
             compiler_params=pltpu.CompilerParams(
-                collective_id=0, has_side_effects=True, vmem_limit_bytes=40 * 1024 * 1024
+                collective_id=0, has_side_effects=True, vmem_limit_bytes=56 * 1024 * 1024
             ),
         )(
             resid,

time: 34.7 us -> 26.4 us (0.76); the launches traced: 34.2 us -> 26.3 us
  local copies, waits for them, and re-layouts: 9.32 us -> 1.23 us
    unnamed x22 -> x2, local copies, waits for them, and re-layouts: 9.32 us -> 1.23 us
where the time goes in v2:
time: 26.4 us; the launch traced here: 26.3 us
  Pallas kernels  24.4 us (92%)
  local copies, waits for them, and re-layouts  1.23 us (5%)
  between operations  0.64 us (2%)
    pallas_call x1, Pallas kernels, per_device(): pl.pallas_call(functools.partial(kernel, n_ctx, n_tp), out_shape=(pltpu.V...  24.4 us
    unnamed x2, local copies, waits for them, and re-layouts  1.23 us

profile of v2, /device:TPU:30, one launch (start us, length us, event | category | flops | bytes accessed | tf_op | source)
XLA Modules:
  0.0 26.3 jit_solution(8833482628973183280)
XLA Ops:
  0.6 24.4 %shard_map.113 = (bf16[128,128]{1,0:T(8,128)(2,1)S(1)}, bf16[128,128]{1,0:T(8,128)(2,1)S(1)}) custom-call(bf16[128,128]{1,0:T(8,128)(2,1)} %resid_hbm.1, bf16[3,128,128]{2,1,0:T(8,128)(2,1)} %bitcast.6, f32[3,3,128]{2,1,0:T(4,128)} %sf_hbm.1, f32[16,128]{1,0:T(8,128)} %bitcast.7, f32[16,128]{1,0:T(8,128)} %bitcast.8, f32[8,128]{1,0:T(8,128)} %bitcast.9, ...), custom_call_target="tpu_custom_call" | custom-call | tf_op jit(solution)/shard_map/pallas_call | solution.py:390
  25.0 0.6 %copy.14 = bf16[128,128]{1,0:T(8,128)(2,1)} copy(bf16[128,128]{1,0:T(8,128)(2,1)S(1)} %get-tuple-element.2) | data formatting | bytes 65536
  25.7 0.6 %copy.15 = bf16[128,128]{1,0:T(8,128)(2,1)} copy(bf16[128,128]{1,0:T(8,128)(2,1)S(1)} %get-tuple-element.3) | data formatting | bytes 65536

commit v3 on v2

--- a/solution.py
+++ b/solution.py
@@ -48,6 +48,8 @@
     fsh,
     msg,
     msg_in,
+    pair_out,
+    pair_in,
     part_out,
     part_in,
     gath,
@@ -63,6 +65,8 @@
     r3,
     s4,
     r4,
+    s5,
+    r5,
 ):
     me_c = lax.axis_index("ctx")
     me_t = lax.axis_index("tp")
@@ -70,6 +74,13 @@
     modes = res_ref.shape[0]
     width = n_tp * 128
     tiles = rows // 8
+    n_chip = n_tp // 2
+    core = lax.rem(me_t, 2)
+    chip = me_t // 2
+    partner = chip * 2 + 1 - core
+
+    def same_core(d):
+        return lax.rem(chip + d, n_chip) * 2 + core
 
     in_copies = []
     for i, (src, dst) in enumerate(
@@ -89,8 +100,7 @@
         c.start()
 
     barrier = pltpu.get_barrier_semaphore()
-    for d in range(1, n_tp):
-        peer = lax.rem(me_t + d, n_tp)
+    for peer in [partner] + [same_core(d) for d in range(1, n_chip)]:
         pl.semaphore_signal(barrier, inc=1, device_id={"tp": peer}, device_id_type=MESH)
     for d in range(1, n_ctx):
 
@@ -143,7 +153,7 @@
         msg[20 + 2 * p : 22 + 2 * p, :] = xpad[p, 8:10, :]
     msg[26:32, :] = jnp.zeros((6, 128), F32)
 
-    pl.semaphore_wait(barrier, n_tp - 1 + (n_ctx - 1 - me_c))
+    pl.semaphore_wait(barrier, n_chip + (n_ctx - 1 - me_c))
 
     def msg_copy(d):
         return pltpu.make_async_remote_copy(
@@ -247,52 +257,80 @@
 
     w_copies[0].wait()
 
-    def part_copy(d, target):
+    def pair_copy(d):
+        return pltpu.make_async_remote_copy(
+            src_ref=pair_out.at[d],
+            dst_ref=pair_in.at[d],
+            send_sem=s5.at[d],
+            recv_sem=r5.at[d],
+            device_id={"tp": partner},
+            device_id_type=MESH,
+        )
+
+    def part_copy(d):
         return pltpu.make_async_remote_copy(
             src_ref=part_out.at[d],
             dst_ref=part_in.at[d],
             send_sem=s2.at[d],
             recv_sem=r2.at[d],
-            device_id={"tp": target},
+            device_id={"tp": same_core(d)},
             device_id_type=MESH,
         )
 
-    def columns(t):
-        return ow[:, pl.ds(pl.multiple_of(t * 128, 128), 128)]
-
-    for d in range(1, n_tp):
-        peer = lax.rem(me_t + d, n_tp)
-        part_out[d] = jnp.dot(gated, columns(peer), preferred_element_type=F32).astype(BF16)
-        part_copy(d, peer).start()
-    mix = jnp.dot(gated, columns(me_t), preferred_element_type=F32)
-    for d in range(1, n_tp):
-        part_copy(d, me_t).wait_recv()
+    def share(t):
+        cols = ow[:, pl.ds(pl.multiple_of(t * 128, 128), 128)]
+        return jnp.dot(gated, cols, preferred_element_type=F32)
+
+    order = list(range(1, n_chip)) + [0]
+    for d in order:
+        pair_out[d] = share(lax.rem(chip + d, n_chip) * 2 + 1 - core)
+        pair_copy(d).start()
+    mine = [share(same_core(d)) for d in order]
+    for d in range(1, n_chip):
+        pair_copy(d).wait_recv()
+        part_out[d] = (mine[d - 1] + pair_in[d]).astype(BF16)
+        part_copy(d).start()
+    pair_copy(0).wait_recv()
+    mix = resid_ref[...].astype(F32) + (mine[-1] + pair_in[0])
+    for d in range(1, n_chip):
+        part_copy(d).wait_recv()
         mix = mix + part_in[d].astype(F32)
-    hyena = (resid_ref[...].astype(F32) + mix).astype(BF16)
+    hyena = mix.astype(BF16)
     gath[me_t] = hyena
 
-    def gath_copy(d, owner, target):
+    def gath_copy(sem, owner, target):
         return pltpu.make_async_remote_copy(
             src_ref=gath.at[owner],
             dst_ref=gath.at[owner],
-            send_sem=s3.at[d],
-            recv_sem=r3.at[d],
+            send_sem=s3.at[sem],
+            recv_sem=r3.at[owner],
             device_id={"tp": target},
             device_id_type=MESH,
         )
 
-    for d in range(1, n_tp):
-        gath_copy(d, me_t, lax.rem(me_t + d, n_tp)).start()
+    for d in range(1, n_chip):
+        gath_copy(d, me_t, same_core(d)).start()
+    gath_copy(0, me_t, partner).start()
     hy_ref[...] = hyena
-    for d in range(1, n_tp):
-        gath_copy(d, lax.rem(me_t + n_tp - d, n_tp), me_t).wait_recv()
-    wide = [gath[j].astype(F32) for j in range(n_tp)]
-    square = wide[0] * wide[0]
-    for j in range(1, n_tp):
-        square = square + wide[j] * wide[j]
+    wide = hyena.astype(F32)
+    square = wide * wide
+    gath_copy(0, partner, partner).wait_recv()
+    wide = gath[partner].astype(F32)
+    square = square + wide * wide
+    for d in range(1, n_chip):
+        owner = same_core(n_chip - d)
+        gath_copy(d, owner, partner).wait_recv()
+        gath_copy(n_chip + d, owner, partner).start()
+        wide = gath[owner].astype(F32)
+        square = square + wide * wide
+    for d in range(1, n_chip):
+        owner = lax.rem(chip + n_chip - d, n_chip) * 2 + 1 - core
+        gath_copy(d, owner, partner).wait_recv()
+        wide = gath[owner].astype(F32)
+        square = square + wide * wide
     scale = lax.rsqrt(jnp.sum(square, axis=1, keepdims=True) / float(width) + EPS)
     normed = jnp.concatenate(
-        [(wide[j] * scale * gain_ref[j : j + 1, :]).astype(BF16) for j in range(n_tp)], axis=1
+        [(gath[j].astype(F32) * scale * gain_ref[j : j + 1, :]).astype(BF16) for j in range(n_tp)], axis=1
     )
     for c in w_copies[1:]:
         c.wait()
@@ -354,9 +392,12 @@
     probs, acc = lax.fori_loop(0, me_c, value_step, (probs, acc))
     ctx_ref[...] = (acc / jnp.sum(probs, axis=1, keepdims=True)).astype(BF16)
 
-    for d in range(1, n_tp):
-        part_copy(d, me_t).wait_send()
-        gath_copy(d, me_t, me_t).wait_send()
+    for d in range(n_chip):
+        pair_copy(d).wait_send()
+        gath_copy(d, me_t, partner).wait_send()
+        if d > 0:
+            part_copy(d).wait_send()
+            gath_copy(n_chip + d, me_t, partner).wait_send()
     for d in range(1, n_ctx):
 
         @pl.when(me_c + d < n_ctx)
@@ -411,8 +452,10 @@
                 pltpu.VMEM((8, 2 * rows, 128), F32),
                 pltpu.VMEM((32, 128), F32),
                 pltpu.VMEM((n_ctx, 32, 128), F32),
-                pltpu.VMEM((n_tp,) + block, BF16),
-                pltpu.VMEM((n_tp,) + block, BF16),
+                pltpu.VMEM((n_tp // 2,) + block, F32),
+                pltpu.VMEM((n_tp // 2,) + block, F32),
+                pltpu.VMEM((n_tp // 2,) + block, BF16),
+                pltpu.VMEM((n_tp // 2,) + block, BF16),
                 pltpu.VMEM((n_tp,) + block, BF16),
                 pltpu.VMEM((2, n_ctx) + block, BF16),
                 pltpu.VMEM((n_ctx,) + block, F32),
@@ -426,6 +469,8 @@
                 dma((n_tp,)),
                 dma((2, n_ctx)),
                 dma((2, n_ctx)),
+                dma((n_tp // 2,)),
+                dma((n_tp // 2,)),
             ],
             compiler_params=pltpu.CompilerParams(
                 collective_id=0, has_side_effects=True, vmem_limit_bytes=56 * 1024 * 1024

time: 26.4 us -> 25.1 us (0.951)
  the two profiles are of different devices: /device:TPU:30 before, /device:TPU:7 now
where the time goes in v3:
time: 25.1 us; the launch traced here: 25 us
  Pallas kernels  23.1 us (92%)
  local copies, waits for them, and re-layouts  1.23 us (5%)
  between operations  0.64 us (3%)
    pallas_call x1, Pallas kernels, per_device(): pl.pallas_call(functools.partial(kernel, n_ctx, n_tp), out_shape=(pltpu.V...  23.1 us
    unnamed x2, local copies, waits for them, and re-layouts  1.23 us

profile of v3, /device:TPU:7, one launch (start us, length us, event | category | flops | bytes accessed | tf_op | source)
XLA Modules:
  0.0 25.0 jit_solution(15708527865401705254)
XLA Ops:
  0.6 23.1 %shard_map.113 = (bf16[128,128]{1,0:T(8,128)(2,1)S(1)}, bf16[128,128]{1,0:T(8,128)(2,1)S(1)}) custom-call(bf16[128,128]{1,0:T(8,128)(2,1)} %resid_hbm.1, bf16[3,128,128]{2,1,0:T(8,128)(2,1)} %bitcast.6, f32[3,3,128]{2,1,0:T(4,128)} %sf_hbm.1, f32[16,128]{1,0:T(8,128)} %bitcast.7, f32[16,128]{1,0:T(8,128)} %bitcast.8, f32[8,128]{1,0:T(8,128)} %bitcast.9, ...), custom_call_target="tpu_custom_call" | custom-call | tf_op jit(solution)/shard_map/pallas_call | solution.py:431
  23.7 0.6 %copy.14 = bf16[128,128]{1,0:T(8,128)(2,1)} copy(bf16[128,128]{1,0:T(8,128)(2,1)S(1)} %get-tuple-element.2) | data formatting | bytes 65536
  24.4 0.6 %copy.15 = bf16[128,128]{1,0:T(8,128)(2,1)} copy(bf16[128,128]{1,0:T(8,128)(2,1)S(1)} %get-tuple-element.3) | data formatting | bytes 65536

commit v4 on v3

--- a/solution.py
+++ b/solution.py
@@ -54,7 +54,6 @@
     part_in,
     gath,
     kv,
-    scores,
     w_sem,
     in_sem,
     s1,
@@ -192,7 +191,23 @@
             acc = acc + fsh[r, pl.ds(start, rows), :] * block[r : r + 1]
         return acc
 
-    conv = lax.fori_loop(0, tiles, conv_step, jnp.zeros((rows, 128), F32))
+    def conv_step_low(j, acc):
+        start = pl.multiple_of(rows + rows // 2 - 8 * j, 8)
+        block = prod[pl.ds(pl.multiple_of(8 * j, 8), 8), :]
+        for r in range(8):
+            acc = acc + fsh[r, pl.ds(start, rows // 2), :] * block[r : r + 1]
+        return acc
+
+    conv = lax.fori_loop(0, tiles // 2, conv_step, jnp.zeros((rows, 128), F32))
+    low = lax.fori_loop(tiles // 2, tiles, conv_step_low, conv[rows // 2 :])
+    conv = jnp.concatenate([conv[: rows // 2], low], axis=0)
+
+    for k in range(1, n_ctx):
+
+        @pl.when(k > me_c)
+        def _(k=k):
+            kv[0, k] = jnp.zeros((rows, 128), BF16)
+            kv[1, k] = jnp.zeros((rows, 128), BF16)
 
     cos_l, sin_l = table_ref[0], table_ref[1]
     cos_b = base_ref[0, pl.ds(me_c, 1), :]
@@ -277,21 +292,19 @@
             device_id_type=MESH,
         )
 
-    def share(t):
-        cols = ow[:, pl.ds(pl.multiple_of(t * 128, 128), 128)]
-        return jnp.dot(gated, cols, preferred_element_type=F32)
-
-    order = list(range(1, n_chip)) + [0]
-    for d in order:
-        pair_out[d] = share(lax.rem(chip + d, n_chip) * 2 + 1 - core)
+    mine = [None] * n_chip
+    for d in list(range(1, n_chip)) + [0]:
+        start = pl.multiple_of(lax.rem(chip + d, n_chip) * 256, 256)
+        both = jnp.dot(gated, ow[:, pl.ds(start, 256)], preferred_element_type=F32)
+        pair_out[d] = jnp.where(core == 0, both[:, 128:256], both[:, 0:128])
         pair_copy(d).start()
-    mine = [share(same_core(d)) for d in order]
+        mine[d] = jnp.where(core == 0, both[:, 0:128], both[:, 128:256])
     for d in range(1, n_chip):
         pair_copy(d).wait_recv()
-        part_out[d] = (mine[d - 1] + pair_in[d]).astype(BF16)
+        part_out[d] = (mine[d] + pair_in[d]).astype(BF16)
         part_copy(d).start()
     pair_copy(0).wait_recv()
-    mix = resid_ref[...].astype(F32) + (mine[-1] + pair_in[0])
+    mix = resid_ref[...].astype(F32) + (mine[0] + pair_in[0])
     for d in range(1, n_chip):
         part_copy(d).wait_recv()
         mix = mix + part_in[d].astype(F32)
@@ -312,35 +325,44 @@
         gath_copy(d, me_t, same_core(d)).start()
     gath_copy(0, me_t, partner).start()
     hy_ref[...] = hyena
-    wide = hyena.astype(F32)
-    square = wide * wide
+    for c in w_copies[1:]:
+        c.wait()
+
+    def chip_block(t, square, key_value, query):
+        scaled = []
+        for i in range(2):
+            wide = gath[2 * t + i].astype(F32)
+            square = square + wide * wide
+            scaled.append((wide * gain_ref[pl.ds(2 * t + i, 1), :]).astype(BF16))
+        scaled = jnp.concatenate(scaled, axis=1)
+        weights = pl.ds(pl.multiple_of(t * 256, 256), 256)
+        key_value = key_value + jnp.dot(scaled, aw[weights, 0:256], preferred_element_type=F32)
+        query = query + jnp.dot(scaled, aw[weights, 256:384], preferred_element_type=F32)
+        return square, key_value, query
+
     gath_copy(0, partner, partner).wait_recv()
-    wide = gath[partner].astype(F32)
-    square = square + wide * wide
+    sums = chip_block(
+        chip,
+        jnp.zeros((rows, 128), F32),
+        jnp.zeros((rows, 256), F32),
+        jnp.zeros((rows, 128), F32),
+    )
     for d in range(1, n_chip):
         owner = same_core(n_chip - d)
         gath_copy(d, owner, partner).wait_recv()
         gath_copy(n_chip + d, owner, partner).start()
-        wide = gath[owner].astype(F32)
-        square = square + wide * wide
     for d in range(1, n_chip):
-        owner = lax.rem(chip + n_chip - d, n_chip) * 2 + 1 - core
-        gath_copy(d, owner, partner).wait_recv()
-        wide = gath[owner].astype(F32)
-        square = square + wide * wide
+        source = lax.rem(chip + n_chip - d, n_chip)
+        gath_copy(d, source * 2 + 1 - core, partner).wait_recv()
+        sums = chip_block(source, *sums)
+    square, key_value, query = sums
     scale = lax.rsqrt(jnp.sum(square, axis=1, keepdims=True) / float(width) + EPS)
-    normed = jnp.concatenate(
-        [(gath[j].astype(F32) * scale * gain_ref[j : j + 1, :]).astype(BF16) for j in range(n_tp)], axis=1
-    )
-    for c in w_copies[1:]:
-        c.wait()
 
     def turned(x):
         return (x * cosine + pltpu.roll(x, 64, axis=1) * sine).astype(BF16)
 
-    key_value = jnp.dot(normed, aw[:, 0:256], preferred_element_type=F32)
-    kv[0, me_c] = turned(key_value[:, 0:128])
-    kv[1, me_c] = key_value[:, 128:256].astype(BF16)
+    kv[0, me_c] = turned(key_value[:, 0:128] * scale)
+    kv[1, me_c] = (key_value[:, 128:256] * scale).astype(BF16)
 
     def kv_copy(which, d, owner, target):
         return pltpu.make_async_remote_copy(
@@ -359,38 +381,38 @@
             def _(which=which, d=d):
                 kv_copy(which, d, me_c, me_c + d).start()
 
-    queries = turned(jnp.dot(normed, aw[:, 256:384], preferred_element_type=F32))
+    queries = turned(query * scale)
     factor = 1.0 / math.sqrt(HEAD_DIM)
-
-    def score_of(k):
-        return (
-            lax.dot_general(
-                queries, kv[0, k], (((1,), (1,)), ((), ())), preferred_element_type=F32
-            )
-            * factor
-        )
-
-    own = jnp.where(row_id >= lane, score_of(me_c), FILL)
-
-    def score_step(k, peak):
-        kv_copy(0, 0, k, k).wait_recv()
-        s = score_of(k)
-        scores[k] = s
-        return jnp.maximum(peak, s)
-
-    peak = jnp.max(lax.fori_loop(0, me_c, score_step, own), axis=1, keepdims=True)
-    probs = jnp.where(row_id >= lane, jnp.exp(own - peak), 0.0)
-    acc = jnp.dot(probs.astype(BF16), kv[1, me_c], preferred_element_type=F32)
-
-    def value_step(k, carried):
-        total_p, total_v = carried
-        kv_copy(1, 0, k, k).wait_recv()
-        pr = jnp.exp(scores[k] - peak)
-        total_v = total_v + jnp.dot(pr.astype(BF16), kv[1, k], preferred_element_type=F32)
-        return total_p + pr, total_v
-
-    probs, acc = lax.fori_loop(0, me_c, value_step, (probs, acc))
-    ctx_ref[...] = (acc / jnp.sum(probs, axis=1, keepdims=True)).astype(BF16)
+    keys_n = n_ctx * rows
+
+    def arrived(which):
+        for k in range(n_ctx - 1):
+
+            @pl.when(k < me_c)
+            def _(k=k):
+                kv_copy(which, 0, k, k).wait_recv()
+
+    row_pos = me_c * rows + lax.broadcasted_iota(jnp.int32, (rows, keys_n), 0)
+    allowed = row_pos >= lax.broadcasted_iota(jnp.int32, (rows, keys_n), 1)
+    arrived(0)
+    scores = (
+        lax.dot_general(
+            queries,
+            kv[0].reshape(keys_n, 128),
+            (((1,), (1,)), ((), ())),
+            preferred_element_type=F32,
+        )
+        * factor
+    )
+    scores = jnp.where(allowed, scores, FILL)
+    probs = jnp.exp(scores - jnp.max(scores, axis=1, keepdims=True))
+    probs = jnp.where(allowed, probs, 0.0)
+    total_p = jnp.sum(probs, axis=1, keepdims=True)
+    arrived(1)
+    acc = jnp.dot(
+        probs.astype(BF16), kv[1].reshape(keys_n, 128), preferred_element_type=F32
+    )
+    ctx_ref[...] = (acc / total_p).astype(BF16)
 
     for d in range(n_chip):
         pair_copy(d).wait_send()
@@ -458,7 +480,6 @@
                 pltpu.VMEM((n_tp // 2,) + block, BF16),
                 pltpu.VMEM((n_tp,) + block, BF16),
                 pltpu.VMEM((2, n_ctx) + block, BF16),
-                pltpu.VMEM((n_ctx,) + block, F32),
                 dma((4,)),
                 dma((8,)),
                 dma((n_ctx,)),

time: 25.1 us -> 24.8 us (0.988); the launches traced: 25 us -> 24.4 us
  Pallas kernels: 23.1 us -> 22.5 us
    pallas_call x1, Pallas kernels: 23.1 us -> 22.5 us  [per_device(): pl.pallas_call(functools.partial(kernel, n_ctx, n_tp), out_shape=(pltpu.V...]
where the time goes in v4:
time: 24.8 us; the launch traced here: 24.4 us
  Pallas kernels  22.5 us (91%)
  local copies, waits for them, and re-layouts  1.23 us (5%)
  between operations  0.64 us (3%)
    pallas_call x1, Pallas kernels, per_device(): pl.pallas_call(functools.partial(kernel, n_ctx, n_tp), out_shape=(pltpu.V...  22.5 us
    unnamed x2, local copies, waits for them, and re-layouts  1.23 us

profile of v4, /device:TPU:7, one launch (start us, length us, event | category | flops | bytes accessed | tf_op | source)
XLA Modules:
  0.0 24.4 jit_solution(14433078172594820463)
XLA Ops:
  0.6 22.5 %shard_map.113 = (bf16[128,128]{1,0:T(8,128)(2,1)S(1)}, bf16[128,128]{1,0:T(8,128)(2,1)S(1)}) custom-call(bf16[128,128]{1,0:T(8,128)(2,1)} %resid_hbm.1, bf16[3,128,128]{2,1,0:T(8,128)(2,1)} %bitcast.6, f32[3,3,128]{2,1,0:T(4,128)} %sf_hbm.1, f32[16,128]{1,0:T(8,128)} %bitcast.7, f32[16,128]{1,0:T(8,128)} %bitcast.8, f32[8,128]{1,0:T(8,128)} %bitcast.9, ...), custom_call_target="tpu_custom_call" | custom-call | tf_op jit(solution)/shard_map/pallas_call | solution.py:453
  23.1 0.6 %copy.14 = bf16[128,128]{1,0:T(8,128)(2,1)} copy(bf16[128,128]{1,0:T(8,128)(2,1)S(1)} %get-tuple-element.2) | data formatting | bytes 65536
  23.8 0.6 %copy.15 = bf16[128,128]{1,0:T(8,128)(2,1)} copy(bf16[128,128]{1,0:T(8,128)(2,1)S(1)} %get-tuple-element.3) | data formatting | bytes 65536

commit v5 on v4

--- a/solution.py
+++ b/solution.py
@@ -272,59 +272,66 @@
 
     w_copies[0].wait()
 
-    def pair_copy(d):
+    half = rows // 2
+
+    def pair_copy(h, d):
         return pltpu.make_async_remote_copy(
-            src_ref=pair_out.at[d],
-            dst_ref=pair_in.at[d],
-            send_sem=s5.at[d],
-            recv_sem=r5.at[d],
+            src_ref=pair_out.at[d, pl.ds(h * half, half)],
+            dst_ref=pair_in.at[d, pl.ds(h * half, half)],
+            send_sem=s5.at[h, d],
+            recv_sem=r5.at[h, d],
             device_id={"tp": partner},
             device_id_type=MESH,
         )
 
-    def part_copy(d):
+    def part_copy(h, d):
         return pltpu.make_async_remote_copy(
-            src_ref=part_out.at[d],
-            dst_ref=part_in.at[d],
-            send_sem=s2.at[d],
-            recv_sem=r2.at[d],
+            src_ref=part_out.at[d, pl.ds(h * half, half)],
+            dst_ref=part_in.at[d, pl.ds(h * half, half)],
+            send_sem=s2.at[h, d],
+            recv_sem=r2.at[h, d],
             device_id={"tp": same_core(d)},
             device_id_type=MESH,
         )
 
-    mine = [None] * n_chip
-    for d in list(range(1, n_chip)) + [0]:
-        start = pl.multiple_of(lax.rem(chip + d, n_chip) * 256, 256)
-        both = jnp.dot(gated, ow[:, pl.ds(start, 256)], preferred_element_type=F32)
-        pair_out[d] = jnp.where(core == 0, both[:, 128:256], both[:, 0:128])
-        pair_copy(d).start()
-        mine[d] = jnp.where(core == 0, both[:, 0:128], both[:, 128:256])
-    for d in range(1, n_chip):
-        pair_copy(d).wait_recv()
-        part_out[d] = (mine[d] + pair_in[d]).astype(BF16)
-        part_copy(d).start()
-    pair_copy(0).wait_recv()
-    mix = resid_ref[...].astype(F32) + (mine[0] + pair_in[0])
-    for d in range(1, n_chip):
-        part_copy(d).wait_recv()
-        mix = mix + part_in[d].astype(F32)
-    hyena = mix.astype(BF16)
-    gath[me_t] = hyena
-
-    def gath_copy(sem, owner, target):
+    def gath_copy(h, sem, owner, target):
         return pltpu.make_async_remote_copy(
-            src_ref=gath.at[owner],
-            dst_ref=gath.at[owner],
-            send_sem=s3.at[sem],
-            recv_sem=r3.at[owner],
+            src_ref=gath.at[owner, pl.ds(h * half, half)],
+            dst_ref=gath.at[owner, pl.ds(h * half, half)],
+            send_sem=s3.at[h, sem],
+            recv_sem=r3.at[h, owner],
             device_id={"tp": target},
             device_id_type=MESH,
         )
 
-    for d in range(1, n_chip):
-        gath_copy(d, me_t, same_core(d)).start()
-    gath_copy(0, me_t, partner).start()
-    hy_ref[...] = hyena
+    mine = [[None] * n_chip for _ in range(2)]
+    for h in range(2):
+        now = slice(h * half, (h + 1) * half)
+        for d in list(range(1, n_chip)) + [0]:
+            start = pl.multiple_of(lax.rem(chip + d, n_chip) * 256, 256)
+            both = jnp.dot(gated[now], ow[:, pl.ds(start, 256)], preferred_element_type=F32)
+            pair_out[d, now] = jnp.where(core == 0, both[:, 128:256], both[:, 0:128])
+            pair_copy(h, d).start()
+            mine[h][d] = jnp.where(core == 0, both[:, 0:128], both[:, 128:256])
+    for h in range(2):
+        now = slice(h * half, (h + 1) * half)
+        for d in range(1, n_chip):
+            pair_copy(h, d).wait_recv()
+            part_out[d, now] = (mine[h][d] + pair_in[d, now]).astype(BF16)
+            part_copy(h, d).start()
+    for h in range(2):
+        now = slice(h * half, (h + 1) * half)
+        pair_copy(h, 0).wait_recv()
+        mix = resid_ref[now].astype(F32) + (mine[h][0] + pair_in[0, now])
+        for d in range(1, n_chip):
+            part_copy(h, d).wait_recv()
+            mix = mix + part_in[d, now].astype(F32)
+        hyena = mix.astype(BF16)
+        gath[me_t, now] = hyena
+        for d in range(1, n_chip):
+            gath_copy(h, d, me_t, same_core(d)).start()
+        gath_copy(h, 0, me_t, partner).start()
+        hy_ref[now] = hyena
     for c in w_copies[1:]:
         c.wait()
 
@@ -340,20 +347,23 @@
         query = query + jnp.dot(scaled, aw[weights, 256:384], preferred_element_type=F32)
         return square, key_value, query
 
-    gath_copy(0, partner, partner).wait_recv()
+    for h in range(2):
+        gath_copy(h, 0, partner, partner).wait_recv()
     sums = chip_block(
         chip,
         jnp.zeros((rows, 128), F32),
         jnp.zeros((rows, 256), F32),
         jnp.zeros((rows, 128), F32),
     )
-    for d in range(1, n_chip):
-        owner = same_core(n_chip - d)
-        gath_copy(d, owner, partner).wait_recv()
-        gath_copy(n_chip + d, owner, partner).start()
+    for h in range(2):
+        for d in range(1, n_chip):
+            owner = same_core(n_chip - d)
+            gath_copy(h, d, owner, partner).wait_recv()
+            gath_copy(h, n_chip + d, owner, partner).start()
     for d in range(1, n_chip):
         source = lax.rem(chip + n_chip - d, n_chip)
-        gath_copy(d, source * 2 + 1 - core, partner).wait_recv()
+        for h in range(2):
+            gath_copy(h, d, source * 2 + 1 - core, partner).wait_recv()
         sums = chip_block(source, *sums)
     square, key_value, query = sums
     scale = lax.rsqrt(jnp.sum(square, axis=1, keepdims=True) / float(width) + EPS)
@@ -414,12 +424,13 @@
     )
     ctx_ref[...] = (acc / total_p).astype(BF16)
 
-    for d in range(n_chip):
-        pair_copy(d).wait_send()
-        gath_copy(d, me_t, partner).wait_send()
-        if d > 0:
-            part_copy(d).wait_send()
-            gath_copy(n_chip + d, me_t, partner).wait_send()
+    for h in range(2):
+        for d in range(n_chip):
+            pair_copy(h, d).wait_send()
+            gath_copy(h, d, me_t, partner).wait_send()
+            if d > 0:
+                part_copy(h, d).wait_send()
+                gath_copy(h, n_chip + d, me_t, partner).wait_send()
     for d in range(1, n_ctx):
 
         @pl.when(me_c + d < n_ctx)
@@ -484,14 +495,14 @@
                 dma((8,)),
                 dma((n_ctx,)),
                 dma((n_ctx,)),
-                dma((n_tp,)),
-                dma((n_tp,)),
-                dma((n_tp,)),
-                dma((n_tp,)),
+                dma((2, n_tp)),
+                dma((2, n_tp)),
+                dma((2, n_tp)),
+                dma((2, n_tp)),
                 dma((2, n_ctx)),
                 dma((2, n_ctx)),
-                dma((n_tp // 2,)),
-                dma((n_tp // 2,)),
+                dma((2, n_tp // 2)),
+                dma((2, n_tp // 2)),
             ],
             compiler_params=pltpu.CompilerParams(
                 collective_id=0, has_side_effects=True, vmem_limit_bytes=56 * 1024 * 1024

time: 24.8 us -> 24.5 us (0.988); the launches traced: 24.4 us -> 24.4 us
  no operation moved by 1% of the time
where the time goes in v5:
time: 24.5 us; the launch traced here: 24.4 us
  Pallas kernels  22.5 us (92%)
  local copies, waits for them, and re-layouts  1.23 us (5%)
  between operations  0.64 us (3%)
    pallas_call x1, Pallas kernels, per_device(): pl.pallas_call(functools.partial(kernel, n_ctx, n_tp), out_shape=(pltpu.V...  22.5 us
    unnamed x2, local copies, waits for them, and re-layouts  1.23 us

profile of v5, /device:TPU:7, one launch (start us, length us, event | category | flops | bytes accessed | tf_op | source)
XLA Modules:
  0.0 24.4 jit_solution(10345438782025927105)
XLA Ops:
  0.6 22.5 %shard_map.113 = (bf16[128,128]{1,0:T(8,128)(2,1)S(1)}, bf16[128,128]{1,0:T(8,128)(2,1)S(1)}) custom-call(bf16[128,128]{1,0:T(8,128)(2,1)} %resid_hbm.1, bf16[3,128,128]{2,1,0:T(8,128)(2,1)} %bitcast.6, f32[3,3,128]{2,1,0:T(4,128)} %sf_hbm.1, f32[16,128]{1,0:T(8,128)} %bitcast.7, f32[16,128]{1,0:T(8,128)} %bitcast.8, f32[8,128]{1,0:T(8,128)} %bitcast.9, ...), custom_call_target="tpu_custom_call" | custom-call | tf_op jit(solution)/shard_map/pallas_call | solution.py:464
  23.1 0.6 %copy.14 = bf16[128,128]{1,0:T(8,128)(2,1)} copy(bf16[128,128]{1,0:T(8,128)(2,1)S(1)} %get-tuple-element.2) | data formatting | bytes 65536
  23.7 0.6 %copy.15 = bf16[128,128]{1,0:T(8,128)(2,1)} copy(bf16[128,128]{1,0:T(8,128)(2,1)S(1)} %get-tuple-element.3) | data formatting | bytes 65536

commit v6 on v5

--- a/solution.py
+++ b/solution.py
@@ -440,6 +440,15 @@
             kv_copy(1, d, me_c, me_c + d).wait_send()
 
 
+def store_kernel(a_ref, b_ref, a_hbm, b_hbm, sem):
+    first = pltpu.make_async_copy(a_ref, a_hbm, sem.at[0])
+    second = pltpu.make_async_copy(b_ref, b_hbm, sem.at[1])
+    first.start()
+    second.start()
+    first.wait()
+    second.wait()
+
+
 def rotary_tables(rows, n_ctx):
     half = HEAD_DIM // 2
     freq = ROPE_BASE ** (-np.arange(half, dtype=np.float64) * 2.0 / HEAD_DIM)
@@ -461,7 +470,7 @@
         hbm = pl.BlockSpec(memory_space=pltpu.HBM)
         dma = pltpu.SemaphoreType.DMA
         block = (rows, 128)
-        return pl.pallas_call(
+        results = pl.pallas_call(
             functools.partial(kernel, n_ctx, n_tp),
             out_shape=(
                 pltpu.VMEM(block, BF16),
@@ -519,6 +528,13 @@
             ow,
             aw.transpose(1, 0, 2),
         )
+        return pl.pallas_call(
+            store_kernel,
+            out_shape=tuple(jax.ShapeDtypeStruct(block, BF16) for _ in range(2)),
+            in_specs=[vmem, vmem],
+            out_specs=(hbm, hbm),
+            scratch_shapes=[dma((2,))],
+        )(*[pltpu.with_memory_space_constraint(x, pltpu.VMEM) for x in results])
 
     in_specs = (
         P("ctx", "tp"),

time: 24.5 us -> 23.9 us (0.976)
  local copies, waits for them, and re-layouts: 1.23 us -> 0 us
  Pallas kernels: 22.5 us -> 23.1 us
    unnamed x2 -> x0, local copies, waits for them, and re-layouts: 1.23 us -> none
    pallas_call x0 -> x1, Pallas kernels: none -> 0.65 us  [per_device(): pl.pallas_call(store_kernel, out_shape=tuple((jax.ShapeDtypeStruct(block,...]
where the time goes in v6:
time: 23.9 us; the launch traced here: 23.8 us
  Pallas kernels  23.1 us (97%)
  between operations  0.64 us (3%)
    pallas_call x1, Pallas kernels, per_device(): pl.pallas_call(functools.partial(kernel, n_ctx, n_tp), out_shape=(pltpu.V...  22.5 us
    pallas_call x1, Pallas kernels, per_device(): pl.pallas_call(store_kernel, out_shape=tuple((jax.ShapeDtypeStruct(block,...  0.65 us

profile of v6, /device:TPU:7, one launch (start us, length us, event | category | flops | bytes accessed | tf_op | source)
XLA Modules:
  0.0 23.8 jit_solution(7365150573434212446)
XLA Ops:
  0.6 22.5 %shard_map.113 = (bf16[128,128]{1,0:T(8,128)(2,1)S(1)}, bf16[128,128]{1,0:T(8,128)(2,1)S(1)}) custom-call(bf16[128,128]{1,0:T(8,128)(2,1)} %resid_hbm.1, bf16[3,128,128]{2,1,0:T(8,128)(2,1)} %bitcast.6, f32[3,3,128]{2,1,0:T(4,128)} %sf_hbm.1, f32[16,128]{1,0:T(8,128)} %bitcast.7, f32[16,128]{1,0:T(8,128)} %bitcast.8, f32[8,128]{1,0:T(8,128)} %bitcast.9, ...), custom_call_target="tpu_custom_call" | custom-call | tf_op jit(solution)/shard_map/pallas_call | solution.py:473
  23.1 0.6 %shard_map.114 = (bf16[128,128]{1,0:T(8,128)(2,1)}, bf16[128,128]{1,0:T(8,128)(2,1)}) custom-call(bf16[128,128]{1,0:T(8,128)(2,1)S(1)} %get-tuple-element.4.a_ref, bf16[128,128]{1,0:T(8,128)(2,1)S(1)} %get-tuple-element.5.b_ref), custom_call_target="tpu_custom_call" | custom-call | tf_op jit(solution)/shard_map/pallas_call | solution.py:531
